TPU v7x, 256 devices: a whole 4x4x8 slice. The times are simulated.
256 devices in a mesh: clip: 8 (over x, y_hi), sy: 8 (over z), sx: 4 (over y_lo, core).
Axes of the slice: x: 4, y: 4 (y_hi: 2, y_lo: 2; y = y_hi * 2 + y_lo), z: 8, core: 2. Of those that a mesh axis runs over, the one named last changes fastest.
Arguments:
- queries: bfloat16 [8, 4, 64, 32, 1536], P('clip', None, 'sy', 'sx'), may hold values from -12 to 12
- keys: bfloat16 [8, 4, 64, 32, 1536], P('clip', None, 'sy', 'sx'), may hold values from -9 to 9
- values: bfloat16 [8, 4, 64, 32, 1536], P('clip', None, 'sy', 'sx'), may hold values from -6 to 6
- cache: bfloat16 [32, 8, 4, 2, 64, 1536], P('clip', 'sy', 'sx'), may hold values from -7 to 7
- ctx_owner: int32 [8, 8, 4, 8], P('clip', 'sy', 'sx'), may hold values from 0 to 7, as said below
- ctx_slot: int32 [8, 8, 4, 8], P('clip', 'sy', 'sx'), may hold values from 0 to 3
- span_count: int32 [8], P('clip'), may hold values from 2 to 4
Outputs:
- attended: bfloat16 [8, 4, 64, 32, 1536], P('clip', None, 'sy', 'sx')
Inputs may be any that keep to these rules, and one draw needn't show every extreme that they name: `ctx_owner`: entries 2 * i to 2 * i + 1 of every tile's list name one owner, and different i name different owners.
All inputs are finite; a program needn't handle non-finite values.
Results may differ from a plain program's by a relative error of at most 0.0033.
Values may be sent and summed in bfloat16 or wider, within the bound.
A program may use at most 128 MiB of HBM per device.

v0:
```python
import math

import jax
import jax.numpy as jnp
from jax import lax
from jax.sharding import PartitionSpec as P

HEAD = 128
REACH = 3
BLK = 64
BPC = 2


def with_halo(block, sides, width):
    for axis, dim in sides:
        count = lax.axis_size(axis)
        forward = [(i, i + 1) for i in range(count - 1)]
        backward = [(target, source) for source, target in forward]
        low = lax.ppermute(
            lax.slice_in_dim(block, block.shape[dim] - width, None, axis=dim), axis, forward
        )
        high = lax.ppermute(lax.slice_in_dim(block, 0, width, axis=dim), axis, backward)
        block = jnp.concatenate([low, block, high], axis=dim)
    return block


def near_mask(tile_len, first_cell, grid_len):
    query_cells = jnp.arange(tile_len, dtype=jnp.int32)
    key_cells = jnp.arange(tile_len + 2 * REACH, dtype=jnp.int32) - REACH
    inside_grid = (key_cells + first_cell >= 0) & (key_cells + first_cell < grid_len)
    return (jnp.abs(query_cells[:, None] - key_cells[None, :]) <= REACH) & inside_grid[None, :]


def per_device(queries, keys, values, cache, ctx_owner, ctx_slot, span_count):
    frames = queries.shape[1]
    tile_rows = queries.shape[2]
    tile_cols = queries.shape[3]
    features = queries.shape[4]
    keys_values = jnp.concatenate([keys, values], 0)
    extended = with_halo(keys_values, (("sy", 2), ("sx", 3)), REACH)
    owners = ctx_owner.reshape(-1)
    slot_ids = ctx_slot.reshape(-1)
    entries = owners.shape[0]
    entry_ids = jnp.arange(entries, dtype=jnp.int32)
    live_mask = entry_ids // BPC < span_count[0]
    owner_count = lax.axis_size("clip")
    capacity = entries // min(owner_count, 4)
    rank_in = entry_ids % capacity
    matches = owners[None, :] == jnp.arange(owner_count, dtype=jnp.int32)[:, None]
    ranked = rank_in[None, :] == jnp.arange(capacity, dtype=jnp.int32)[:, None]
    placed = matches[:, None, :] & ranked[None, :, :]
    wanted = jnp.where(live_mask, slot_ids, -1)
    request = jnp.sum(jnp.where(placed, wanted[None, None, :] + 1, 0), axis=2) - 1
    blocks_here = cache.reshape(cache.shape[0], 2, BLK, features)
    asked_for = lax.all_to_all(request, "clip", split_axis=0, concat_axis=0, tiled=True)
    clamped = jnp.clip(asked_for, 0, blocks_here.shape[0] - 1)
    fetched = jnp.take(blocks_here, clamped, axis=0)
    fetched = jnp.where(
        (asked_for >= 0)[:, :, None, None, None], fetched, jnp.zeros((), fetched.dtype)
    )
    replies = lax.all_to_all(fetched, "clip", split_axis=0, concat_axis=0, tiled=True)
    flattened = replies.reshape(-1, 2, BLK, features)
    context = jnp.take(flattened, owners * capacity + rank_in, axis=0)
    key_flat = jnp.concatenate(
        [extended[0].reshape(-1, features), context[:, 0].reshape(-1, features)], 0
    )
    value_flat = jnp.concatenate(
        [extended[1].reshape(-1, features), context[:, 1].reshape(-1, features)], 0
    )
    row_first = lax.axis_index("sy") * tile_rows
    col_first = lax.axis_index("sx") * tile_cols
    near_rows = near_mask(tile_rows, row_first, lax.axis_size("sy") * tile_rows)
    near_cols = near_mask(tile_cols, col_first, lax.axis_size("sx") * tile_cols)
    plane_mask = (near_rows[:, None, :, None] & near_cols[None, :, None, :]).reshape(
        tile_rows * tile_cols, -1
    )
    query_count = frames * tile_rows * tile_cols
    local_mask = jnp.broadcast_to(
        plane_mask[None, :, None, :], (frames, tile_rows * tile_cols, frames, plane_mask.shape[1])
    ).reshape(query_count, -1)
    context_mask = jnp.broadcast_to(
        jnp.repeat(live_mask, BLK)[None, :], (query_count, entries * BLK)
    )
    allowed = jnp.concatenate([local_mask, context_mask], 1)
    query_flat = queries.reshape(query_count, features)
    head_count = features // HEAD
    per_group = min(4, head_count)
    score_scale = 1.0 / math.sqrt(HEAD)
    results = []
    for first_head in range(0, head_count, per_group):
        finish = min(first_head + per_group, head_count)
        lower = first_head * HEAD
        upper = finish * HEAD
        group_size = finish - first_head
        query_group = query_flat[:, lower:upper].reshape(query_count, group_size, HEAD)
        key_group = key_flat[:, lower:upper].reshape(-1, group_size, HEAD)
        value_group = value_flat[:, lower:upper].reshape(-1, group_size, HEAD)
        scores = (
            jnp.einsum("qhd,khd->hqk", query_group, key_group, preferred_element_type=jnp.float32)
            * score_scale
        )
        scores = jnp.where(allowed[None], scores, jnp.float32(-1e30))
        highest = jnp.max(scores, axis=2, keepdims=True)
        unnormed = jnp.exp(scores - highest)
        totals = jnp.sum(unnormed, axis=2)
        mixture = jnp.einsum(
            "hqk,khd->qhd",
            unnormed.astype(jnp.bfloat16),
            value_group,
            preferred_element_type=jnp.float32,
        )
        mixture = mixture / jnp.transpose(totals)[:, :, None]
        results.append(mixture.reshape(query_count, group_size * HEAD))
    attended = jnp.concatenate(results, 1).astype(jnp.bfloat16)
    return attended.reshape(queries.shape)


def solution(mesh):
    placed = (
        P("clip", None, "sy", "sx", None),
        P("clip", None, "sy", "sx", None),
        P("clip", None, "sy", "sx", None),
        P("clip", "sy", "sx", None, None, None),
        P("clip", "sy", "sx", None),
        P("clip", "sy", "sx", None),
        P("clip"),
    )
    return jax.shard_map(
        per_device,
        mesh=mesh,
        in_specs=placed,
        out_specs=P("clip", None, "sy", "sx", None),
        check_vma=False,
    )
```

profile of v0, /device:TPU:120, one launch (start us, length us, event | category | flops | bytes accessed | tf_op | source)
XLA Modules:
  0.0 161.0 jit_solution(9828850679967400351)
XLA Ops:
  2.3 11.8 %all_to_all.11 = s32[8,1,2]{2,1,0:T(1,128)S(1)} all-to-all(s32[8,1,2]{2,1,0:T(1,128)S(1)} %copy.160), channel_id=1, replica_groups=mesh['clip'=8,'sy'=8,'sx'=4] {'clip'}, dimensions={0} | all-to-all | bytes 128 | tf_op jit(solution)/shard_map/all_to_all | solution.py:55
  14.6 3.6 %gather_fusion = bf16[16,2,64,1536]{3,2,1,0:T(8,128)(2,1)} fusion(bf16[4,2,64,1536]{3,2,1,0:T(8,128)(2,1)S(1)} %bitcast.118, s32[1024]{0:T(1024)S(1)} %pad_clamp_fusion.1), kind=kCustom, calls=%fused_computation | custom fusion | bytes 12582976 | tf_op jit(solution)/shard_map/jit(_take)/gather | solution.py:57
  18.2 6.2 %select_select_fusion = bf16[8,2,2,64,1536]{4,3,2,1,0:T(8,128)(2,1)} fusion(bf16[8,2,2,64,1536]{4,3,2,1,0:T(8,128)(2,1)} %bitcast.119, pred[8,2]{1,0:T(8,128)(4,1)S(1)} %copy.164, pred[8,2]{1,0:T(8,128)(4,1)S(1)} %copy.162), kind=kLoop, calls=%fused_computation.2 | loop fusion | flops 6291456 | bytes 12582944 | tf_op jit(solution)/shard_map/jit(_where)/select_n | solution.py:58
  24.4 7.7 %all-to-all-start.1 = ((bf16[8,2,2,64,1536]{4,3,2,1,0:T(8,128)(2,1)}), bf16[8,2,2,64,1536]{4,3,2,1,0:T(8,128)(2,1)}, u32[]{:S(2)}, u32[]{:S(2)}) async-start(bf16[8,2,2,64,1536]{4,3,2,1,0:T(8,128)(2,1)} %select_select_fusion), calls=%async_computation.1 | async-start | bytes 12582912 | tf_op jit(solution)/shard_map/all_to_all | solution.py:61
  33.4 5.0 %collective-permute-start = (bf16[2,4,3,8,1536]{4,3,2,1,0:T(8,128)(2,1)}, bf16[2,4,3,8,1536]{4,3,2,1,0:T(8,128)(2,1)S(1)}, u32[]{:S(2)}, u32[]{:S(2)}) collective-permute-start(bf16[2,4,3,8,1536]{4,3,2,1,0:T(8,128)(2,1)} %get-tuple-element.17), channel_id=1, source_target_pairs={{0,4},{4,8},{8,12},{12,16},{16,20},{20,24},{24,28},{1,5},{5,9},{9,... | collective-permute-start | bytes 1769480 | tf_op jit(solution)/shard_map/ppermute | solution.py:19
  38.4 1.9 %collective-permute-start.1 = (bf16[2,4,3,8,1536]{4,3,2,1,0:T(8,128)(2,1)}, bf16[2,4,3,8,1536]{4,3,2,1,0:T(8,128)(2,1)S(1)}, u32[]{:S(2)}, u32[]{:S(2)}) collective-permute-start(bf16[2,4,3,8,1536]{4,3,2,1,0:T(8,128)(2,1)} %get-tuple-element.18), channel_id=1, source_target_pairs={{4,0},{8,4},{12,8},{16,12},{20,16},{24,20},{28,24},{5,1},{9,5},{13... | collective-permute-start | bytes 1769480 | tf_op jit(solution)/shard_map/ppermute | solution.py:22
  41.6 7.9 %collective-permute-done = bf16[2,4,3,8,1536]{4,3,2,1,0:T(8,128)(2,1)S(1)} collective-permute-done((bf16[2,4,3,8,1536]{4,3,2,1,0:T(8,128)(2,1)}, bf16[2,4,3,8,1536]{4,3,2,1,0:T(8,128)(2,1)S(1)}, u32[]{:S(2)}, u32[]{:S(2)}) %collective-permute-start) | collective-permute-done | bytes 589856 | tf_op jit(solution)/shard_map/ppermute | solution.py:19
  49.6 5.2 %collective-permute-done.1 = bf16[2,4,3,8,1536]{4,3,2,1,0:T(8,128)(2,1)S(1)} collective-permute-done((bf16[2,4,3,8,1536]{4,3,2,1,0:T(8,128)(2,1)}, bf16[2,4,3,8,1536]{4,3,2,1,0:T(8,128)(2,1)S(1)}, u32[]{:S(2)}, u32[]{:S(2)}) %collective-permute-start.1) | collective-permute-done | bytes 589856 | tf_op jit(solution)/shard_map/ppermute | solution.py:22
  57.3 1.9 %collective-permute-start.2 = (bf16[2,4,14,3,1536]{4,2,3,1,0:T(8,128)(2,1)}, bf16[2,4,14,3,1536]{4,2,3,1,0:T(8,128)(2,1)}, u32[]{:S(2)}, u32[]{:S(2)}) collective-permute-start(bf16[2,4,14,3,1536]{4,2,3,1,0:T(8,128)(2,1)} %copy.156), channel_id=1, source_target_pairs={{0,1},{1,2},{2,3},{4,5},{5,6},{6,7},{8,9},{9,10},{10,11},{12,13},{... | collective-permute-start | bytes 3096584 | tf_op jit(solution)/shard_map/ppermute | solution.py:19
  60.6 3.9 %collective-permute-start.3 = (bf16[2,4,14,3,1536]{4,2,3,1,0:T(8,128)(2,1)}, bf16[2,4,14,3,1536]{4,2,3,1,0:T(8,128)(2,1)}, u32[]{:S(2)}, u32[]{:S(2)}) collective-permute-start(bf16[2,4,14,3,1536]{4,2,3,1,0:T(8,128)(2,1)} %copy.157), channel_id=1, source_target_pairs={{1,0},{2,1},{3,2},{5,4},{6,5},{7,6},{9,8},{10,9},{11,10},{13,12},{... | collective-permute-start | bytes 3096584 | tf_op jit(solution)/shard_map/ppermute | solution.py:22
  69.6 42.6 %collective-permute-done.2 = bf16[2,4,14,3,1536]{4,2,3,1,0:T(8,128)(2,1)} collective-permute-done((bf16[2,4,14,3,1536]{4,2,3,1,0:T(8,128)(2,1)}, bf16[2,4,14,3,1536]{4,2,3,1,0:T(8,128)(2,1)}, u32[]{:S(2)}, u32[]{:S(2)}) %collective-permute-start.2) | collective-permute-done | bytes 1032224 | tf_op jit(solution)/shard_map/ppermute | solution.py:19
  112.2 2.2 %copy.158 = bf16[2,4,14,3,1536]{4,3,2,1,0:T(4,128)(2,1)S(1)} copy(bf16[2,4,14,3,1536]{4,2,3,1,0:T(8,128)(2,1)} %collective-permute-done.2) | data formatting | bytes 2064384 | tf_op jit(solution)/shard_map/ppermute | solution.py:19
  114.3 2.2 %copy.159 = bf16[2,4,14,3,1536]{4,3,2,1,0:T(4,128)(2,1)S(1)} copy(bf16[2,4,14,3,1536]{4,2,3,1,0:T(8,128)(2,1)} %collective-permute-done.3) | data formatting | bytes 2064384 | tf_op jit(solution)/shard_map/ppermute | solution.py:22
  116.5 4.2 %pad_maximum_fusion = bf16[2,4,14,14,1536]{4,3,2,1,0:T(8,128)(2,1)S(1)} fusion(bf16[2,4,14,3,1536]{4,3,2,1,0:T(4,128)(2,1)S(1)} %copy.159, bf16[2,4,3,8,1536]{4,3,2,1,0:T(8,128)(2,1)S(1)} %collective-permute-done.1, bf16[2,4,8,8,1536]{4,3,2,1,0:T(8,128)(2,1)S(1)} %constant_dynamic-update-slice_fusion, ...), kind=kLoop, calls=%fused_computation.3 | loop fusion | flops 24084480 | bytes 9633792 | tf_op jit(solution)/shard_map/concatenate | solution.py:23
  120.8 2.8 %fusion.88 = (bf16[1,4,14,14,1536]{4,3,2,1,0:T(8,128)(2,1)}, bf16[1,4,14,14,1536]{4,3,2,1,0:T(8,128)(2,1)}) fusion(bf16[2,4,14,14,1536]{4,3,2,1,0:T(8,128)(2,1)S(1)} %pad_maximum_fusion), kind=kLoop, calls=%fused_computation.100 | loop fusion | bytes 9633792 | tf_op jit(solution)/shard_map/slice | solution.py:68
  123.6 4.9 %reshape_squeeze.14 = bf16[784,1536]{1,0:T(8,128)(2,1)} reshape(bf16[1,4,14,14,1536]{4,3,2,1,0:T(8,128)(2,1)} %get-tuple-element.6) | data formatting | bytes 4816896 | tf_op jit(solution)/shard_map/reshape;squeeze | solution.py:65
  128.5 4.9 %reshape_squeeze.12 = bf16[784,1536]{1,0:T(8,128)(2,1)} reshape(bf16[1,4,14,14,1536]{4,3,2,1,0:T(8,128)(2,1)} %get-tuple-element.5) | data formatting | bytes 4816896 | tf_op jit(solution)/shard_map/reshape;squeeze | solution.py:68
  133.4 5.2 %gather_fusion.1 = bf16[8,2,64,1536]{3,2,1,0:T(8,128)(2,1)} fusion(bf16[16,2,64,1536]{3,2,1,0:T(8,128)(2,1)} %bitcast.9, s32[1024]{0:T(1024)S(1)} %pad_clamp_fusion), kind=kCustom, calls=%fused_computation.1 | custom fusion | bytes 6291488 | tf_op jit(solution)/shard_map/jit(_take)/gather | solution.py:63
  138.6 2.3 %broadcast_select_fusion = bf16[8,2,64,1536]{3,2,1,0:T(8,128)(2,1)S(1)} fusion(bf16[8,2,64,1536]{3,2,1,0:T(8,128)(2,1)} %gather_fusion.1, pred[8]{0:T(512)(128)(4,1)S(1)} %compare_and_fusion.3), kind=kLoop, calls=%fused_computation.24 | loop fusion | flops 1572864 | bytes 6291464 | tf_op jit(solution)/shard_map/jit(_take)/select_n | solution.py:63
  141.2 1.4 copy-done.3
  142.6 1.7 %fusion.18 = (bf16[162,4,8,128]{3,2,1,0:T(8,128)(2,1)S(1)}, bf16[162,4,8,128]{3,2,1,0:T(8,128)(2,1)S(1)}, bf16[162,4,8,128]{3,2,1,0:T(8,128)(2,1)}) fusion(bf16[784,1536]{1,0:T(8,128)(2,1)S(1)} %copy-done.3, bf16[512,1536]{1,0:T(8,128)(2,1)S(1)} %bitcast.121), kind=kLoop, calls=%fused_computation.36 | loop fusion | flops 7962624 | bytes 7962624
  147.0 2.1 %fusion.22 = (bf16[162,4,8,128]{3,2,1,0:T(8,128)(2,1)S(1)}, bf16[162,4,8,128]{3,2,1,0:T(8,128)(2,1)}, bf16[162,4,8,128]{3,2,1,0:T(8,128)(2,1)}) fusion(bf16[784,1536]{1,0:T(8,128)(2,1)S(1)} %copy-done.2, bf16[512,1536]{1,0:T(8,128)(2,1)S(1)} %bitcast.120), kind=kLoop, calls=%fused_computation.40 | loop fusion | flops 7962624 | bytes 7962624
  150.5 2.0 %fusion.94 = (f32[4,256]{1,0:T(4,128)S(1)}, f32[4,256,1296]{1,2,0:T(8,128)S(1)}) fusion(bf16[256,4,128]{0,2,1:T(8,128)(2,1)} %bitcast.124, bf16[162,4,8,128]{3,2,1,0:T(8,128)(2,1)S(1)} %copy-done.5, pred[256,1296]{0,1:T(8,128)(4,1)} %copy.166), kind=kOutput, calls=%fused_computation.106 | convolution fusion | flops 343718912 | bytes 7233536 | tf_op jit(solution)/shard_map/qhd,khd->hqk/dot_general | solution.py:99
  155.3 2.0 %fusion.93 = (f32[4,256]{1,0:T(4,128)S(1)}, f32[4,256,1296]{1,2,0:T(8,128)S(1)}) fusion(bf16[256,4,128]{0,2,1:T(8,128)(2,1)} %bitcast.123, bf16[162,4,8,128]{3,2,1,0:T(8,128)(2,1)S(1)} %get-tuple-element.11, pred[256,1296]{0,1:T(8,128)(4,1)} %copy.166), kind=kOutput, calls=%fused_computation.105 | convolution fusion | flops 343718912 | bytes 7233536 | tf_op jit(solution)/shard_map/qhd,khd->hqk/dot_general | solution.py:99
  (83 shorter events, 24.0 us)
Async XLA Ops:
  0.0 14.6 %copy-start = (bf16[4,1,1,2,64,1536]{5,4,3,2,1,0:T(8,128)(2,1)S(1)}, bf16[4,1,1,2,64,1536]{5,4,3,2,1,0:T(8,128)(2,1)}, u32[]{:S(2)}) copy-start(bf16[4,1,1,2,64,1536]{5,4,3,2,1,0:T(8,128)(2,1)} %param.10) | copy-start | bytes 4718596
  24.4 7.7 %copy-start.7 = (bf16[1,4,8,8,1536]{4,3,2,1,0:T(8,128)(2,1)S(1)}, bf16[1,4,8,8,1536]{4,3,2,1,0:T(8,128)(2,1)}, u32[]{:S(2)}) copy-start(bf16[1,4,8,8,1536]{4,3,2,1,0:T(8,128)(2,1)} %param.8) | copy-start | bytes 2359300
  24.4 7.8 %copy-start.8 = (bf16[1,4,8,8,1536]{4,3,2,1,0:T(8,128)(2,1)S(1)}, bf16[1,4,8,8,1536]{4,3,2,1,0:T(8,128)(2,1)}, u32[]{:S(2)}) copy-start(bf16[1,4,8,8,1536]{4,3,2,1,0:T(8,128)(2,1)} %param.9) | copy-start | bytes 2359300
  24.4 109.0 %all-to-all-start.1 = ((bf16[8,2,2,64,1536]{4,3,2,1,0:T(8,128)(2,1)}), bf16[8,2,2,64,1536]{4,3,2,1,0:T(8,128)(2,1)}, u32[]{:S(2)}, u32[]{:S(2)}) async-start(bf16[8,2,2,64,1536]{4,3,2,1,0:T(8,128)(2,1)} %select_select_fusion), calls=%async_computation.1 | async-start | bytes 12582912 | tf_op jit(solution)/shard_map/all_to_all | solution.py:61
  33.4 16.2 %collective-permute-start = (bf16[2,4,3,8,1536]{4,3,2,1,0:T(8,128)(2,1)}, bf16[2,4,3,8,1536]{4,3,2,1,0:T(8,128)(2,1)S(1)}, u32[]{:S(2)}, u32[]{:S(2)}) collective-permute-start(bf16[2,4,3,8,1536]{4,3,2,1,0:T(8,128)(2,1)} %get-tuple-element.17), channel_id=1, source_target_pairs={{0,4},{4,8},{8,12},{12,16},{16,20},{20,24},{24,28},{1,5},{5,9},{9,... | collective-permute-start | bytes 1769480 | tf_op jit(solution)/shard_map/ppermute | solution.py:19
  38.4 16.4 %collective-permute-start.1 = (bf16[2,4,3,8,1536]{4,3,2,1,0:T(8,128)(2,1)}, bf16[2,4,3,8,1536]{4,3,2,1,0:T(8,128)(2,1)S(1)}, u32[]{:S(2)}, u32[]{:S(2)}) collective-permute-start(bf16[2,4,3,8,1536]{4,3,2,1,0:T(8,128)(2,1)} %get-tuple-element.18), channel_id=1, source_target_pairs={{4,0},{8,4},{12,8},{16,12},{20,16},{24,20},{28,24},{5,1},{9,5},{13... | collective-permute-start | bytes 1769480 | tf_op jit(solution)/shard_map/ppermute | solution.py:22
  57.3 54.8 %collective-permute-start.2 = (bf16[2,4,14,3,1536]{4,2,3,1,0:T(8,128)(2,1)}, bf16[2,4,14,3,1536]{4,2,3,1,0:T(8,128)(2,1)}, u32[]{:S(2)}, u32[]{:S(2)}) collective-permute-start(bf16[2,4,14,3,1536]{4,2,3,1,0:T(8,128)(2,1)} %copy.156), channel_id=1, source_target_pairs={{0,1},{1,2},{2,3},{4,5},{5,6},{6,7},{8,9},{9,10},{10,11},{12,13},{... | collective-permute-start | bytes 3096584 | tf_op jit(solution)/shard_map/ppermute | solution.py:19
  60.6 9.0 %copy-start.11 = (s32[1,1,1,8]{3,2,1,0:T(1,128)S(1)}, s32[1,1,1,8]{3,2,1,0:T(1,128)}, u32[]{:S(2)}) copy-start(s32[1,1,1,8]{3,2,1,0:T(1,128)} %param.11) | copy-start | bytes 100
  60.6 53.7 %collective-permute-start.3 = (bf16[2,4,14,3,1536]{4,2,3,1,0:T(8,128)(2,1)}, bf16[2,4,14,3,1536]{4,2,3,1,0:T(8,128)(2,1)}, u32[]{:S(2)}, u32[]{:S(2)}) collective-permute-start(bf16[2,4,14,3,1536]{4,2,3,1,0:T(8,128)(2,1)} %copy.157), channel_id=1, source_target_pairs={{1,0},{2,1},{3,2},{5,4},{6,5},{7,6},{9,8},{10,9},{11,10},{13,12},{... | collective-permute-start | bytes 3096584 | tf_op jit(solution)/shard_map/ppermute | solution.py:22
  140.9 1.7 %copy-start.3 = (bf16[784,1536]{1,0:T(8,128)(2,1)S(1)}, bf16[784,1536]{1,0:T(8,128)(2,1)}, u32[]{:S(2)}) copy-start(bf16[784,1536]{1,0:T(8,128)(2,1)} %reshape_squeeze.14) | copy-start | bytes 7225348
  142.6 1.7 %copy-start.9 = (pred[256,1296]{0,1:T(8,128)(4,1)S(1)}, pred[256,1296]{0,1:T(8,128)(4,1)}, u32[]{:S(2)}) copy-start(pred[256,1296]{0,1:T(8,128)(4,1)} %copy.166) | copy-start | bytes 995332
  142.6 1.7 %copy-start.10 = (bf16[256,512]{0,1:T(8,128)(2,1)S(1)}, bf16[256,512]{0,1:T(8,128)(2,1)}, u32[]{:S(2)}) copy-start(bf16[256,512]{0,1:T(8,128)(2,1)} %copy.167) | copy-start | bytes 786436
  145.3 1.7 %copy-start.2 = (bf16[784,1536]{1,0:T(8,128)(2,1)S(1)}, bf16[784,1536]{1,0:T(8,128)(2,1)}, u32[]{:S(2)}) copy-start(bf16[784,1536]{1,0:T(8,128)(2,1)} %reshape_squeeze.12) | copy-start | bytes 7225348
  149.1 1.4 copy-start.5
  152.6 1.3 copy-start.6
  157.3 1.3 copy-start.4
  158.7 2.3 %copy-start.1 = (bf16[4,1,1,2,64,1536]{5,4,3,2,1,0:T(8,128)(2,1)S(1)}, bf16[4,1,1,2,64,1536]{5,4,3,2,1,0:T(8,128)(2,1)}, u32[]{:S(2)}) copy-start(bf16[4,1,1,2,64,1536]{5,4,3,2,1,0:T(8,128)(2,1)} %param.10) | copy-start | bytes 4718596
where the time goes:
time: 162 us; the launch traced here: 161 us
  waiting for transfers between devices  55.8 us (34%)
  local copies, waits for them, and re-layouts  41.7 us (26%)
  other arithmetic  21.8 us (13%)
  starting transfers between devices  20.5 us (13%)
  blocking collectives  11.8 us (7%)
  matrix products  8.31 us (5%)
    ppermute x2, waiting for transfers between devices, with_halo(): lax.ppermute(lax.slice_in_dim(block, block.shape[dim] - width, None, axis...  50.5 us
    all_to_all x1, blocking collectives, per_device(): lax.all_to_all(request, 'clip', split_axis=0, concat_axis=0, tiled=True)  11.8 us
    all_to_all x1, starting transfers between devices, per_device(): lax.all_to_all(fetched, 'clip', split_axis=0, concat_axis=0, tiled=True)  7.7 us
    ppermute x2, starting transfers between devices, with_halo(): lax.ppermute(lax.slice_in_dim(block, block.shape[dim] - width, None, axis...  6.93 us
    select_n x1, other arithmetic, per_device(): jnp.where((asked_for >= 0)[:, :, None, None, None], fetched, jnp.zeros(()...  6.18 us
    ppermute x2, starting transfers between devices, with_halo(): lax.ppermute(lax.slice_in_dim(block, 0, width, axis=dim), axis, backward)  5.86 us
    gather x1, local copies, waits for them, and re-layouts, per_device(): context = jnp.take(flattened, owners * capacity + rank_in, axis=0)  5.24 us
    ppermute x2, waiting for transfers between devices, with_halo(): lax.ppermute(lax.slice_in_dim(block, 0, width, axis=dim), axis, backward)  5.22 us
  transfers between devices with their start and end apart: 5, of which 3 were waited for; matrix products, arithmetic and copies ran while one was open for 20% of the time, Pallas kernels for 0%

commit v1 on v0

v1 whole, which is shorter than its diff:
```python
import functools
import math

import jax
import jax.numpy as jnp
from jax import lax
from jax.experimental import pallas as pl
from jax.experimental.pallas import tpu as pltpu
from jax.sharding import PartitionSpec as P

HEAD = 128
HEADS = 12
HD = HEAD * HEADS
REACH = 3
BLK = 64
BPC = 2
CTX = 8
SLOTS = 4
FRAMES = 4
QN = 256
STRIP = 192
CHUNKS = 3
CW = HD // CHUNKS
LEAD = 2
FIRST_OWN = 7
NONE = -1e30
FLOOR = -1e29
RATE = math.log2(math.e) / math.sqrt(HEAD)
TWICE = 1.0 / RATE
MESH = pl.DeviceIdType.MESH
NT = (((1,), (1,)), ((), ()))
TN = (((0,), (0,)), ((), ()))


def dot(a, b, dims):
    return lax.dot_general(a, b, dims, preferred_element_type=jnp.float32)


def kernel(
    owner_ref, slot_ref, span_ref, q_hbm, k_hbm, v_hbm, cache_hbm, out_hbm,
    land, q_own, q_far, kv_own, kv_up, kv_dn, strip_out, strip_in, select, mask,
    bias_own, bias_out, bias_far, part_out, part_in, out_buf,
    cache_sem, q_sem, kv_sem, own_ss, own_rs, fwd_ss, fwd_rs, qs, qr, ps, pr,
    bias_ss, bias_rs, row_ss, row_rs, col_ss, col_rs, out_sem,
):
    clip = lax.axis_index("clip")
    sy = lax.axis_index("sy")
    sx = lax.axis_index("sx")
    rows_n = lax.axis_size("sy")
    cols_n = lax.axis_size("sx")
    x = clip // 2
    yh = clip % 2
    x_next = (lax.rem(clip + 2, 8), sy, sx)
    x_prev = (lax.rem(clip + 6, 8), sy, sx)
    across = (clip + 1 - 2 * yh, sy, sx)
    row_next = (clip, lax.rem(sy + 1, rows_n), sx)
    row_prev = (clip, lax.rem(sy + rows_n - 1, rows_n), sx)
    col_next = (clip, sy, lax.rem(sx + 1, cols_n))
    col_prev = (clip, sy, lax.rem(sx + cols_n - 1, cols_n))

    def lanes(h, width=HEAD):
        return pl.ds(pl.multiple_of(h * width, HEAD), width)

    def cache_copy(h):
        return pltpu.make_async_copy(cache_hbm.at[:, :, :, lanes(h)], land.at[h, 0], cache_sem.at[h])

    def q_copy(h):
        return pltpu.make_async_copy(q_hbm.at[:, lanes(h)], q_own.at[h], q_sem.at[h])

    def out_copy(h):
        return pltpu.make_async_copy(out_buf.at[h], out_hbm.at[:, lanes(h)], out_sem.at[h])

    k_copy = pltpu.make_async_copy(k_hbm, kv_own.at[0], kv_sem.at[0])
    v_copy = pltpu.make_async_copy(v_hbm, kv_own.at[1], kv_sem.at[1])

    def remote(src, dst, ss, rs, device):
        return pltpu.make_async_remote_copy(
            src_ref=src, dst_ref=dst, send_sem=ss, recv_sem=rs, device_id=device, device_id_type=MESH
        )

    def own_send(h, way):
        return remote(
            land.at[h, 0], land.at[h, 1 + way], own_ss.at[way, h], own_rs.at[way, h], (x_next, x_prev)[way]
        )

    def forward(h, way):
        half = pl.ds(2 * way, 2)
        return remote(
            land.at[h, 1 + way, half], land.at[h, 3, half], fwd_ss.at[way, h], fwd_rs.at[way, h],
            (x_next, x_prev)[way],
        )

    def q_send(h):
        return remote(q_own.at[h], q_far.at[h], qs.at[h], qr.at[h], across)

    def part_send(h):
        return remote(part_out.at[h], part_in.at[h], ps.at[h], pr.at[h], across)

    bias_send = remote(bias_out, bias_far, bias_ss, bias_rs, across)

    def row_send(c, way):
        rows = pl.ds(32 * (1 - way), 32)
        return remote(
            kv_own.at[:, :, rows, lanes(c, CW)], (kv_up, kv_dn)[way].at[c], row_ss.at[way, c], row_rs.at[way, c],
            (row_next, row_prev)[way],
        )

    def col_send(c, way):
        return remote(
            strip_out.at[way, c], strip_in.at[way, c], col_ss.at[way, c], col_rs.at[way, c],
            (col_next, col_prev)[way],
        )

    row_has = (sy > 0, sy < rows_n - 1)
    row_to = (sy < rows_n - 1, sy > 0)
    col_has = (sx > 0, sx < cols_n - 1)
    col_to = (sx < cols_n - 1, sx > 0)

    def start_local(h, carry):
        cache_copy(h).start()
        q_copy(h).start()
        return carry

    barrier = pltpu.get_barrier_semaphore()
    for device in (x_next, x_prev, across, row_next, row_prev, col_next, col_prev):
        pl.semaphore_signal(barrier, inc=1, device_id=device, device_id_type=MESH)
    k_copy.start()
    v_copy.start()
    lax.fori_loop(0, HEADS, start_local, 0)

    place = lax.broadcasted_iota(jnp.int32, (16, QN), 0)
    source = place >> 2
    step = jnp.where(source == 0, 0, jnp.where(source == 1, 3, jnp.where(source == 2, 1, 2)))
    base = ((x + step) & 3) * (2 * SLOTS) + (place & 3)
    for ref, half in ((bias_own, yh), (bias_out, 1 - yh)):
        target = base + half * SLOTS
        count = jnp.zeros((16, QN), jnp.int32)
        for j in range(CTX):
            listed = owner_ref[j] * SLOTS + slot_ref[j]
            listed = jnp.where(j // BPC < span_ref[0], listed, -1)
            count = count + jnp.where(target == listed, 1, 0)
        ref[...] = jnp.where(count == 0, NONE, jnp.where(count == 1, 0.0, TWICE)).astype(jnp.float32)

    pl.semaphore_wait(barrier, 7)
    for h in range(LEAD):
        cache_copy(h).wait()
        own_send(h, 0).start()
        own_send(h, 1).start()
        q_copy(h).wait()
        q_send(h).start()
        if h == 0:
            bias_send.start()
    k_copy.wait()
    v_copy.wait()
    for c in range(CHUNKS):
        for way in range(2):
            pl.when(row_to[way])(row_send(c, way).start)

    for way, ref in ((0, kv_up), (1, kv_dn)):

        @pl.when(jnp.logical_not(row_has[way]))
        def _():
            ref[...] = jnp.zeros_like(ref)

    for way in range(2):

        @pl.when(jnp.logical_not(col_has[way]))
        def _():
            strip_in[way] = jnp.zeros(strip_in.shape[1:], strip_in.dtype)

    strip_row = lax.broadcasted_iota(jnp.int32, (STRIP, 512), 0)
    from_row = lax.broadcasted_iota(jnp.int32, (STRIP, 512), 1)
    frame = (strip_row >> 4) & 3
    height = strip_row & 15
    for way in range(2):
        column = (strip_row >> 6) + (5 if way == 0 else 0)
        wanted = jnp.where(
            height < 4,
            256 + frame * 32 + height * 8,
            jnp.where(height < 12, frame * 64 + (height - 4) * 8, 384 + frame * 32 + (height - 12) * 8),
        )
        select[way] = jnp.where(wanted + column == from_row, 1.0, 0.0).astype(jnp.bfloat16)

    def mask_part(first, count, row_col):
        r = lax.broadcasted_iota(jnp.int32, (count, QN), 0)
        query = lax.broadcasted_iota(jnp.int32, (count, QN), 1)
        row, col = row_col(r)
        down = row - ((query >> 3) & 7)
        right = col - (query & 7)
        row_at = row + sy * 8
        col_at = col + sx * 8
        near = (down <= REACH) & (down >= -REACH) & (right <= REACH) & (right >= -REACH)
        inside = (row_at >= 0) & (row_at < rows_n * 8) & (col_at >= 0) & (col_at < cols_n * 8)
        mask[first : first + count, :] = jnp.where(near & inside, 0.0, NONE).astype(jnp.float32)

    mask_part(0, 256, lambda r: ((r >> 3) & 7, r & 7))
    mask_part(256, 128, lambda r: (((r >> 3) & 3) - 4, r & 7))
    mask_part(384, 128, lambda r: (((r >> 3) & 3) + 8, r & 7))
    mask_part(512, STRIP, lambda r: ((r & 15) - 4, (r >> 6) - 3))
    mask_part(512 + STRIP, STRIP, lambda r: ((r & 15) - 4, (r >> 6) + 8))

    def ring_scores(h, query, bias):
        scores, highest = [], jnp.full((1, QN), FLOOR, jnp.float32)
        for r in range(4):
            s = dot(land[h, r, :, 0].reshape(QN, HEAD), query, NT)
            for b in range(4):
                top = jnp.max(s[b * BLK : (b + 1) * BLK], axis=0, keepdims=True)
                highest = jnp.maximum(highest, top + bias[4 * r + b : 4 * r + b + 1])
            scores.append(s)
        return scores, highest

    def ring_sums(h, scores, highest, bias, total, mixed):
        for r in range(4):
            shift = [highest - bias[4 * r + b : 4 * r + b + 1] for b in range(4)]
            p = jnp.concatenate(
                [jnp.exp2((scores[r][b * BLK : (b + 1) * BLK] - shift[b]) * RATE) for b in range(4)], 0
            )
            total = total + jnp.sum(p, axis=0, keepdims=True)
            mixed = mixed + dot(land[h, r, :, 1].reshape(QN, HEAD), p.astype(jnp.bfloat16), TN)
        return total, mixed

    def attend_far(h):
        bias = bias_far[...]
        scores, highest = ring_scores(h, q_far[h], bias)
        highest = highest.astype(jnp.bfloat16).astype(jnp.float32)
        total, mixed = ring_sums(
            h, scores, highest, bias, jnp.zeros((1, QN), jnp.float32), jnp.zeros((HEAD, QN), jnp.float32)
        )
        coarse = total.astype(jnp.bfloat16).astype(jnp.float32)
        row = lax.broadcasted_iota(jnp.int32, (16, QN), 0)
        stats = jnp.where(row == 0, highest, jnp.where(row == 1, coarse, total - coarse))
        part_out[h, :HEAD] = mixed.astype(jnp.bfloat16)
        part_out[h, HEAD:] = stats.astype(jnp.bfloat16)

    def attend_own(h):
        query = q_own[h]
        bias = bias_own[...]
        c = h // (HEADS // CHUNKS)
        here = lanes(h - c * (HEADS // CHUNKS))

        def pieces(kv):
            own = kv_own[kv, :, :, lanes(h)].reshape(QN, HEAD)
            up = kv_up[c, kv, :, :, here].reshape(128, HEAD)
            dn = kv_dn[c, kv, :, :, here].reshape(128, HEAD)
            left = strip_in[0, c, kv, :, here]
            right = strip_in[1, c, kv, :, here]
            return own, jnp.concatenate([up, dn], 0), jnp.concatenate([left, right], 0)

        scores, highest = ring_scores(h, query, bias)
        near, first = [], 0
        for piece in pieces(0):
            s = dot(piece, query, NT) + mask[first : first + piece.shape[0], :]
            first += piece.shape[0]
            highest = jnp.maximum(highest, jnp.max(s, axis=0, keepdims=True))
            near.append(s)
        total, mixed = ring_sums(
            h, scores, highest, bias, jnp.zeros((1, QN), jnp.float32), jnp.zeros((HEAD, QN), jnp.float32)
        )
        for piece, s in zip(pieces(1), near):
            p = jnp.exp2((s - highest) * RATE)
            total = total + jnp.sum(p, axis=0, keepdims=True)
            mixed = mixed + dot(piece, p.astype(jnp.bfloat16), TN)
        part_send(h).wait_recv()
        stats = part_in[h, HEAD:].astype(jnp.float32)
        far_highest, far_total = stats[0:1], stats[1:2] + stats[2:3]
        top = jnp.maximum(highest, far_highest)
        here_scale = jnp.exp2((highest - top) * RATE)
        far_scale = jnp.exp2((far_highest - top) * RATE)
        inverse = 1.0 / (total * here_scale + far_total * far_scale)
        result = mixed * (here_scale * inverse) + part_in[h, :HEAD].astype(jnp.float32) * (far_scale * inverse)
        out_buf[h] = result.T.astype(jnp.bfloat16)
        out_copy(h).start()

    def make_strips(c):
        for way in range(2):
            pl.when(row_has[way])(row_send(c, way).wait_recv)
        for kv in range(2):
            tile = kv_own[kv, :, :, lanes(c, CW)].reshape(QN, CW)
            halo = jnp.concatenate([kv_up[c, kv].reshape(128, CW), kv_dn[c, kv].reshape(128, CW)], 0)
            for way in range(2):
                packed = jnp.dot(select[way, :, :QN], tile, preferred_element_type=jnp.float32)
                packed = packed + jnp.dot(select[way, :, QN:], halo, preferred_element_type=jnp.float32)
                strip_out[way, c, kv] = packed.astype(jnp.bfloat16)
        for way in range(2):
            pl.when(col_to[way])(col_send(c, way).start)

    def ring_step(h, carry):
        @pl.when(h < HEADS)
        def _():
            for way in range(2):
                own_send(h, way).wait_recv()
                forward(h, way).start()

        @pl.when(h + LEAD < HEADS)
        def _():
            cache_copy(h + LEAD).wait()
            own_send(h + LEAD, 0).start()
            own_send(h + LEAD, 1).start()
            q_copy(h + LEAD).wait()
            q_send(h + LEAD).start()

        @pl.when((h >= 2) & (h < 2 + CHUNKS))
        def _():
            make_strips(h - 2)

        @pl.when(h >= 1)
        def _():
            for way in range(2):
                forward(h - 1, way).wait_recv()
            q_send(h - 1).wait_recv()
            pl.when(h == 1)(bias_send.wait_recv)
            attend_far(h - 1)
            part_send(h - 1).start()

        @pl.when(h >= FIRST_OWN)
        def _():
            first = 2 * (h - FIRST_OWN)

            @pl.when(lax.rem(first, HEADS // CHUNKS) == 0)
            def _():
                for way in range(2):
                    pl.when(col_has[way])(col_send(first // (HEADS // CHUNKS), way).wait_recv)

            def own_step(i, carry):
                attend_own(first + i)
                return carry

            lax.fori_loop(0, 2, own_step, 0)

        return carry

    lax.fori_loop(0, HEADS + 1, ring_step, 0)

    def finish(h, carry):
        for way in range(2):
            own_send(h, way).wait_send()
            forward(h, way).wait_send()
        q_send(h).wait_send()
        part_send(h).wait_send()
        out_copy(h).wait()
        return carry

    lax.fori_loop(0, HEADS, finish, 0)
    bias_send.wait_send()
    for c in range(CHUNKS):
        for way in range(2):
            pl.when(row_to[way])(row_send(c, way).wait_send)
            pl.when(col_to[way])(col_send(c, way).wait_send)


def per_device(queries, keys, values, cache, ctx_owner, ctx_slot, span_count):
    bf16, f32, dma = jnp.bfloat16, jnp.float32, pltpu.SemaphoreType.DMA
    smem = pl.BlockSpec(memory_space=pltpu.SMEM)
    anywhere = pl.BlockSpec(memory_space=pl.ANY)
    attended = pl.pallas_call(
        kernel,
        out_shape=jax.ShapeDtypeStruct((QN, HD), bf16),
        in_specs=[smem] * 3 + [anywhere] * 4,
        out_specs=anywhere,
        scratch_shapes=[
            pltpu.VMEM((HEADS, 4, SLOTS, 2, BLK, HEAD), bf16),
            pltpu.VMEM((HEADS, QN, HEAD), bf16),
            pltpu.VMEM((HEADS, QN, HEAD), bf16),
            pltpu.VMEM((2, FRAMES, 64, HD), bf16),
            pltpu.VMEM((CHUNKS, 2, FRAMES, 32, CW), bf16),
            pltpu.VMEM((CHUNKS, 2, FRAMES, 32, CW), bf16),
            pltpu.VMEM((2, CHUNKS, 2, STRIP, CW), bf16),
            pltpu.VMEM((2, CHUNKS, 2, STRIP, CW), bf16),
            pltpu.VMEM((2, STRIP, 512), bf16),
            pltpu.VMEM((512 + 2 * STRIP, QN), f32),
            pltpu.VMEM((16, QN), f32),
            pltpu.VMEM((16, QN), f32),
            pltpu.VMEM((16, QN), f32),
            pltpu.VMEM((HEADS, HEAD + 16, QN), bf16),
            pltpu.VMEM((HEADS, HEAD + 16, QN), bf16),
            pltpu.VMEM((HEADS, QN, HEAD), bf16),
            dma((HEADS,)), dma((HEADS,)), dma((2,)),
            dma((2, HEADS)), dma((2, HEADS)), dma((2, HEADS)), dma((2, HEADS)),
            dma((HEADS,)), dma((HEADS,)), dma((HEADS,)), dma((HEADS,)),
            dma, dma,
            dma((2, CHUNKS)), dma((2, CHUNKS)), dma((2, CHUNKS)), dma((2, CHUNKS)),
            dma((HEADS,)),
        ],
        compiler_params=pltpu.CompilerParams(
            collective_id=0, has_side_effects=True, vmem_limit_bytes=60 * 2**20
        ),
        cost_estimate=pl.CostEstimate(flops=4 * QN * 2944 * HD, bytes_accessed=6 * 2**20, transcendentals=QN * 2944 * HEADS),
        name="span_attention",
    )(
        ctx_owner.reshape(-1),
        ctx_slot.reshape(-1),
        span_count.reshape(-1),
        queries.reshape(QN, HD),
        keys.reshape(FRAMES, 64, HD),
        values.reshape(FRAMES, 64, HD),
        cache.reshape(SLOTS, 2, BLK, HD),
    )
    return attended.reshape(queries.shape)


def solution(mesh):
    placed = (
        P("clip", None, "sy", "sx", None),
        P("clip", None, "sy", "sx", None),
        P("clip", None, "sy", "sx", None),
        P("clip", "sy", "sx", None, None, None),
        P("clip", "sy", "sx", None),
        P("clip", "sy", "sx", None),
        P("clip"),
    )
    return jax.shard_map(
        per_device,
        mesh=mesh,
        in_specs=placed,
        out_specs=P("clip", None, "sy", "sx", None),
        check_vma=False,
    )
```

time: 162 us -> 76.8 us (0.47)
  the two profiles are of different devices: /device:TPU:120 before, /device:TPU:24 now
where the time goes in v1:
time: 76.8 us; the launch traced here: 76.7 us
  Pallas kernels  74 us (96%)
  local copies, waits for them, and re-layouts  2.06 us (3%)
    pallas_call x1, Pallas kernels, per_device(): pl.pallas_call(kernel, out_shape=jax.ShapeDtypeStruct((QN, HD), bf16), in...  74 us
    unnamed x1, local copies, waits for them, and re-layouts  2.06 us

profile of v1, /device:TPU:24, one launch (start us, length us, event | category | flops | bytes accessed | tf_op | source)
XLA Modules:
  0.0 76.7 jit_solution(9678947460451710890)
XLA Ops:
  0.7 74.0 %span_attention.1 = bf16[256,1536]{1,0:T(8,128)(2,1)} custom-call(s32[8]{0:T(128)} %bitcast.12, s32[8]{0:T(128)} %bitcast.13, s32[1]{0:T(128)S(6)} %copy.9.span_ref, bf16[256,1536]{1,0:T(8,128)(2,1)} %bitcast.9, bf16[4,64,1536]{2,1,0:T(8,128)(2,1)} %bitcast.10, bf16[4,64,1536]{2,1,0:T(8,128)(2,1)} %bitcast.11, bf16[4,2,64,1536]{3,2,1,0:T(8,128)(2,1)} %bitcast.8), custom_call_target="tpu_custom_call" | custom-call | flops 4630511616 | bytes 6291456 | tf_op jit(solution)/shard_map/span_attention/pallas_call | solution.py:355
  74.6 2.1 %copy.10 = bf16[1,4,8,8,1536]{4,3,2,1,0:T(8,128)(2,1)} copy(bf16[1,4,8,8,1536]{4,3,2,1,0:T(8,128)(2,1)} %bitcast.7) | data formatting | bytes 1572864

commit v2 on v1

--- a/solution.py
+++ b/solution.py
@@ -21,10 +21,12 @@
 STRIP = 192
 CHUNKS = 3
 CW = HD // CHUNKS
-LEAD = 2
-FIRST_OWN = 7
+LEAD = 3
+LAG = 2
+MERGE_LAG = 2
+FIRST_OWN = 5
 NONE = -1e30
-FLOOR = -1e29
+FLOOR = -(2.0**96)
 RATE = math.log2(math.e) / math.sqrt(HEAD)
 TWICE = 1.0 / RATE
 MESH = pl.DeviceIdType.MESH
@@ -37,11 +39,11 @@
 
 
 def kernel(
-    owner_ref, slot_ref, span_ref, q_hbm, k_hbm, v_hbm, cache_hbm, out_hbm,
+    owner_ref, slot_ref, span_ref, q_hbm, k_hbm, v_hbm, cache_hbm, out_ref,
     land, q_own, q_far, kv_own, kv_up, kv_dn, strip_out, strip_in, select, mask,
-    bias_own, bias_out, bias_far, part_out, part_in, out_buf,
+    bias_own, bias_out, bias_far, part_out, part_in, far_sum, far_stat, own_sum, own_stat,
     cache_sem, q_sem, kv_sem, own_ss, own_rs, fwd_ss, fwd_rs, qs, qr, ps, pr,
-    bias_ss, bias_rs, row_ss, row_rs, col_ss, col_rs, out_sem,
+    bias_ss, bias_rs, row_ss, row_rs, col_ss, col_rs,
 ):
     clip = lax.axis_index("clip")
     sy = lax.axis_index("sy")
@@ -67,9 +69,6 @@
     def q_copy(h):
         return pltpu.make_async_copy(q_hbm.at[:, lanes(h)], q_own.at[h], q_sem.at[h])
 
-    def out_copy(h):
-        return pltpu.make_async_copy(out_buf.at[h], out_hbm.at[:, lanes(h)], out_sem.at[h])
-
     k_copy = pltpu.make_async_copy(k_hbm, kv_own.at[0], kv_sem.at[0])
     v_copy = pltpu.make_async_copy(v_hbm, kv_own.at[1], kv_sem.at[1])
 
@@ -116,17 +115,27 @@
     col_has = (sx > 0, sx < cols_n - 1)
     col_to = (sx < cols_n - 1, sx > 0)
 
+    barrier = pltpu.get_barrier_semaphore()
+
+    def greet(device):
+        pl.semaphore_signal(barrier, inc=1, device_id=device, device_id_type=MESH)
+
+    for device in (x_next, x_prev, across):
+        greet(device)
+    for way, device in ((0, row_next), (1, row_prev)):
+        pl.when(row_to[way])(functools.partial(greet, device))
+    for way, device in ((0, col_next), (1, col_prev)):
+        pl.when(col_to[way])(functools.partial(greet, device))
+
     def start_local(h, carry):
         cache_copy(h).start()
         q_copy(h).start()
         return carry
 
-    barrier = pltpu.get_barrier_semaphore()
-    for device in (x_next, x_prev, across, row_next, row_prev, col_next, col_prev):
-        pl.semaphore_signal(barrier, inc=1, device_id=device, device_id_type=MESH)
+    lax.fori_loop(0, LEAD, start_local, 0)
     k_copy.start()
     v_copy.start()
-    lax.fori_loop(0, HEADS, start_local, 0)
+    lax.fori_loop(LEAD, HEADS, start_local, 0)
 
     place = lax.broadcasted_iota(jnp.int32, (16, QN), 0)
     source = place >> 2
@@ -141,7 +150,8 @@
             count = count + jnp.where(target == listed, 1, 0)
         ref[...] = jnp.where(count == 0, NONE, jnp.where(count == 1, 0.0, TWICE)).astype(jnp.float32)
 
-    pl.semaphore_wait(barrier, 7)
+    neighbours = [jnp.where(has, 1, 0) for has in row_has + col_has]
+    pl.semaphore_wait(barrier, 3 + sum(neighbours))
     for h in range(LEAD):
         cache_copy(h).wait()
         own_send(h, 0).start()
@@ -156,30 +166,31 @@
         for way in range(2):
             pl.when(row_to[way])(row_send(c, way).start)
 
-    for way, ref in ((0, kv_up), (1, kv_dn)):
-
-        @pl.when(jnp.logical_not(row_has[way]))
-        def _():
-            ref[...] = jnp.zeros_like(ref)
-
-    for way in range(2):
-
-        @pl.when(jnp.logical_not(col_has[way]))
-        def _():
-            strip_in[way] = jnp.zeros(strip_in.shape[1:], strip_in.dtype)
-
-    strip_row = lax.broadcasted_iota(jnp.int32, (STRIP, 512), 0)
-    from_row = lax.broadcasted_iota(jnp.int32, (STRIP, 512), 1)
-    frame = (strip_row >> 4) & 3
-    height = strip_row & 15
-    for way in range(2):
-        column = (strip_row >> 6) + (5 if way == 0 else 0)
-        wanted = jnp.where(
-            height < 4,
-            256 + frame * 32 + height * 8,
-            jnp.where(height < 12, frame * 64 + (height - 4) * 8, 384 + frame * 32 + (height - 12) * 8),
-        )
-        select[way] = jnp.where(wanted + column == from_row, 1.0, 0.0).astype(jnp.bfloat16)
+    def fill_edges_and_select():
+        for way, ref in ((0, kv_up), (1, kv_dn)):
+
+            @pl.when(jnp.logical_not(row_has[way]))
+            def _():
+                ref[...] = jnp.zeros_like(ref)
+
+        for way in range(2):
+
+            @pl.when(jnp.logical_not(col_has[way]))
+            def _():
+                strip_in[way] = jnp.zeros(strip_in.shape[1:], strip_in.dtype)
+
+        strip_row = lax.broadcasted_iota(jnp.int32, (STRIP, 512), 0)
+        from_row = lax.broadcasted_iota(jnp.int32, (STRIP, 512), 1)
+        frame = (strip_row >> 4) & 3
+        height = strip_row & 15
+        for way in range(2):
+            column = (strip_row >> 6) + (5 if way == 0 else 0)
+            wanted = jnp.where(
+                height < 4,
+                256 + frame * 32 + height * 8,
+                jnp.where(height < 12, frame * 64 + (height - 4) * 8, 384 + frame * 32 + (height - 12) * 8),
+            )
+            select[way] = jnp.where(wanted + column == from_row, 1.0, 0.0).astype(jnp.bfloat16)
 
     def mask_part(first, count, row_col):
         r = lax.broadcasted_iota(jnp.int32, (count, QN), 0)
@@ -193,15 +204,16 @@
         inside = (row_at >= 0) & (row_at < rows_n * 8) & (col_at >= 0) & (col_at < cols_n * 8)
         mask[first : first + count, :] = jnp.where(near & inside, 0.0, NONE).astype(jnp.float32)
 
-    mask_part(0, 256, lambda r: ((r >> 3) & 7, r & 7))
-    mask_part(256, 128, lambda r: (((r >> 3) & 3) - 4, r & 7))
-    mask_part(384, 128, lambda r: (((r >> 3) & 3) + 8, r & 7))
-    mask_part(512, STRIP, lambda r: ((r & 15) - 4, (r >> 6) - 3))
-    mask_part(512 + STRIP, STRIP, lambda r: ((r & 15) - 4, (r >> 6) + 8))
-
-    def ring_scores(h, query, bias):
+    def make_mask():
+        mask_part(0, 256, lambda r: ((r >> 3) & 7, r & 7))
+        mask_part(256, 128, lambda r: (((r >> 3) & 3) - 4, r & 7))
+        mask_part(384, 128, lambda r: (((r >> 3) & 3) + 8, r & 7))
+        mask_part(512, STRIP, lambda r: ((r & 15) - 4, (r >> 6) - 3))
+        mask_part(512 + STRIP, STRIP, lambda r: ((r & 15) - 4, (r >> 6) + 8))
+
+    def ring_scores(h, query, bias, blocks):
         scores, highest = [], jnp.full((1, QN), FLOOR, jnp.float32)
-        for r in range(4):
+        for r in blocks:
             s = dot(land[h, r, :, 0].reshape(QN, HEAD), query, NT)
             for b in range(4):
                 top = jnp.max(s[b * BLK : (b + 1) * BLK], axis=0, keepdims=True)
@@ -209,23 +221,34 @@
             scores.append(s)
         return scores, highest
 
-    def ring_sums(h, scores, highest, bias, total, mixed):
-        for r in range(4):
+    def ring_sums(h, scores, highest, bias, blocks, total, mixed):
+        for r, s in zip(blocks, scores):
             shift = [highest - bias[4 * r + b : 4 * r + b + 1] for b in range(4)]
-            p = jnp.concatenate(
-                [jnp.exp2((scores[r][b * BLK : (b + 1) * BLK] - shift[b]) * RATE) for b in range(4)], 0
-            )
+            p = jnp.concatenate([jnp.exp2((s[b * BLK : (b + 1) * BLK] - shift[b]) * RATE) for b in range(4)], 0)
             total = total + jnp.sum(p, axis=0, keepdims=True)
             mixed = mixed + dot(land[h, r, :, 1].reshape(QN, HEAD), p.astype(jnp.bfloat16), TN)
         return total, mixed
 
-    def attend_far(h):
+    def no_sum():
+        return jnp.zeros((1, QN), jnp.float32), jnp.zeros((HEAD, QN), jnp.float32)
+
+    def far_early(h):
         bias = bias_far[...]
-        scores, highest = ring_scores(h, q_far[h], bias)
-        highest = highest.astype(jnp.bfloat16).astype(jnp.float32)
-        total, mixed = ring_sums(
-            h, scores, highest, bias, jnp.zeros((1, QN), jnp.float32), jnp.zeros((HEAD, QN), jnp.float32)
-        )
+        scores, highest = ring_scores(h, q_far[h], bias, (0, 1, 2))
+        total, mixed = ring_sums(h, scores, highest, bias, (0, 1, 2), *no_sum())
+        at = lax.rem(h, LAG + 1)
+        far_sum[at] = mixed
+        far_stat[at, 0:1] = highest
+        far_stat[at, 1:2] = total
+
+    def far_late(h):
+        bias = bias_far[...]
+        at = lax.rem(h, LAG + 1)
+        early_highest, early_total = far_stat[at, 0:1], far_stat[at, 1:2]
+        scores, highest = ring_scores(h, q_far[h], bias, (3,))
+        highest = jnp.maximum(highest, early_highest).astype(jnp.bfloat16).astype(jnp.float32)
+        early = jnp.exp2((early_highest - highest) * RATE)
+        total, mixed = ring_sums(h, scores, highest, bias, (3,), early_total * early, far_sum[at] * early)
         coarse = total.astype(jnp.bfloat16).astype(jnp.float32)
         row = lax.broadcasted_iota(jnp.int32, (16, QN), 0)
         stats = jnp.where(row == 0, highest, jnp.where(row == 1, coarse, total - coarse))
@@ -246,30 +269,34 @@
             right = strip_in[1, c, kv, :, here]
             return own, jnp.concatenate([up, dn], 0), jnp.concatenate([left, right], 0)
 
-        scores, highest = ring_scores(h, query, bias)
+        blocks = (0, 1, 2, 3)
+        scores, highest = ring_scores(h, query, bias, blocks)
         near, first = [], 0
         for piece in pieces(0):
             s = dot(piece, query, NT) + mask[first : first + piece.shape[0], :]
             first += piece.shape[0]
             highest = jnp.maximum(highest, jnp.max(s, axis=0, keepdims=True))
             near.append(s)
-        total, mixed = ring_sums(
-            h, scores, highest, bias, jnp.zeros((1, QN), jnp.float32), jnp.zeros((HEAD, QN), jnp.float32)
-        )
+        total, mixed = ring_sums(h, scores, highest, bias, blocks, *no_sum())
         for piece, s in zip(pieces(1), near):
             p = jnp.exp2((s - highest) * RATE)
             total = total + jnp.sum(p, axis=0, keepdims=True)
             mixed = mixed + dot(piece, p.astype(jnp.bfloat16), TN)
+        own_sum[h] = mixed
+        own_stat[h, 0:1] = highest
+        own_stat[h, 1:2] = total
+
+    def merge(h):
         part_send(h).wait_recv()
         stats = part_in[h, HEAD:].astype(jnp.float32)
         far_highest, far_total = stats[0:1], stats[1:2] + stats[2:3]
+        highest, total = own_stat[h, 0:1], own_stat[h, 1:2]
         top = jnp.maximum(highest, far_highest)
         here_scale = jnp.exp2((highest - top) * RATE)
         far_scale = jnp.exp2((far_highest - top) * RATE)
         inverse = 1.0 / (total * here_scale + far_total * far_scale)
-        result = mixed * (here_scale * inverse) + part_in[h, :HEAD].astype(jnp.float32) * (far_scale * inverse)
-        out_buf[h] = result.T.astype(jnp.bfloat16)
-        out_copy(h).start()
+        result = own_sum[h] * (here_scale * inverse) + part_in[h, :HEAD].astype(jnp.float32) * (far_scale * inverse)
+        out_ref[:, lanes(h)] = result.T.astype(jnp.bfloat16)
 
     def make_strips(c):
         for way in range(2):
@@ -299,37 +326,50 @@
             q_copy(h + LEAD).wait()
             q_send(h + LEAD).start()
 
+        pl.when(h == 0)(fill_edges_and_select)
+        pl.when(h == 1)(make_mask)
+
         @pl.when((h >= 2) & (h < 2 + CHUNKS))
         def _():
             make_strips(h - 2)
 
-        @pl.when(h >= 1)
+        @pl.when(h >= LAG)
         def _():
             for way in range(2):
-                forward(h - 1, way).wait_recv()
-            q_send(h - 1).wait_recv()
-            pl.when(h == 1)(bias_send.wait_recv)
-            attend_far(h - 1)
-            part_send(h - 1).start()
-
-        @pl.when(h >= FIRST_OWN)
+                forward(h - LAG, way).wait_recv()
+            far_late(h - LAG)
+            part_send(h - LAG).start()
+
+        @pl.when(h < HEADS)
         def _():
-            first = 2 * (h - FIRST_OWN)
-
-            @pl.when(lax.rem(first, HEADS // CHUNKS) == 0)
+            q_send(h).wait_recv()
+            pl.when(h == 0)(bias_send.wait_recv)
+            far_early(h)
+
+        def merge_step(i, carry):
+            merge(i)
+            return carry
+
+        def own_step(i, carry):
+            @pl.when(lax.rem(i, HEADS // CHUNKS) == 0)
             def _():
                 for way in range(2):
-                    pl.when(col_has[way])(col_send(first // (HEADS // CHUNKS), way).wait_recv)
-
-            def own_step(i, carry):
-                attend_own(first + i)
-                return carry
-
-            lax.fori_loop(0, 2, own_step, 0)
-
+                    pl.when(col_has[way])(col_send(i // (HEADS // CHUNKS), way).wait_recv)
+
+            attend_own(i)
+            return carry
+
+        lax.fori_loop(own_done(h - MERGE_LAG), own_done(h - MERGE_LAG + 1), merge_step, 0)
+        lax.fori_loop(own_done(h), own_done(h + 1), own_step, 0)
         return carry
 
-    lax.fori_loop(0, HEADS + 1, ring_step, 0)
+    def own_done(step):
+        return jnp.clip(2 * (step - FIRST_OWN), 0, jnp.maximum(step - LAG, 0))
+
+    steps = HEADS + LAG
+    lax.fori_loop(0, steps, ring_step, 0)
+    for h in range(min(2 * (steps - MERGE_LAG - FIRST_OWN), HEADS - MERGE_LAG), HEADS):
+        merge(h)
 
     def finish(h, carry):
         for way in range(2):
@@ -337,7 +377,6 @@
             forward(h, way).wait_send()
         q_send(h).wait_send()
         part_send(h).wait_send()
-        out_copy(h).wait()
         return carry
 
     lax.fori_loop(0, HEADS, finish, 0)
@@ -354,9 +393,9 @@
     anywhere = pl.BlockSpec(memory_space=pl.ANY)
     attended = pl.pallas_call(
         kernel,
-        out_shape=jax.ShapeDtypeStruct((QN, HD), bf16),
+        out_shape=pltpu.VMEM((QN, HD), bf16),
         in_specs=[smem] * 3 + [anywhere] * 4,
-        out_specs=anywhere,
+        out_specs=pl.BlockSpec(memory_space=pltpu.VMEM),
         scratch_shapes=[
             pltpu.VMEM((HEADS, 4, SLOTS, 2, BLK, HEAD), bf16),
             pltpu.VMEM((HEADS, QN, HEAD), bf16),
@@ -373,13 +412,15 @@
             pltpu.VMEM((16, QN), f32),
             pltpu.VMEM((HEADS, HEAD + 16, QN), bf16),
             pltpu.VMEM((HEADS, HEAD + 16, QN), bf16),
-            pltpu.VMEM((HEADS, QN, HEAD), bf16),
+            pltpu.VMEM((LAG + 1, HEAD, QN), f32),
+            pltpu.VMEM((LAG + 1, 8, QN), f32),
+            pltpu.VMEM((HEADS, HEAD, QN), f32),
+            pltpu.VMEM((HEADS, 8, QN), f32),
             dma((HEADS,)), dma((HEADS,)), dma((2,)),
             dma((2, HEADS)), dma((2, HEADS)), dma((2, HEADS)), dma((2, HEADS)),
             dma((HEADS,)), dma((HEADS,)), dma((HEADS,)), dma((HEADS,)),
             dma, dma,
             dma((2, CHUNKS)), dma((2, CHUNKS)), dma((2, CHUNKS)), dma((2, CHUNKS)),
-            dma((HEADS,)),
         ],
         compiler_params=pltpu.CompilerParams(
             collective_id=0, has_side_effects=True, vmem_limit_bytes=60 * 2**20

time: 76.8 us -> 70 us (0.911)
  the two profiles are of different devices: /device:TPU:24 before, /device:TPU:96 now
where the time goes in v2:
time: 70 us; the launch traced here: 69.9 us
  Pallas kernels  68.4 us (98%)
  local copies, waits for them, and re-layouts  0.88 us (1%)
    pallas_call x1, Pallas kernels, per_device(): pl.pallas_call(kernel, out_shape=pltpu.VMEM((QN, HD), bf16), in_specs=[sm...  68.4 us

profile of v2, /device:TPU:96, one launch (start us, length us, event | category | flops | bytes accessed | tf_op | source)
XLA Modules:
  0.0 69.9 jit_solution(17192776080894067942)
XLA Ops:
  0.7 68.4 %span_attention.1 = bf16[256,1536]{1,0:T(8,128)(2,1)S(1)} custom-call(s32[8]{0:T(128)} %bitcast.12, s32[8]{0:T(128)} %bitcast.13, s32[1]{0:T(128)S(6)} %copy.10.span_ref, bf16[256,1536]{1,0:T(8,128)(2,1)} %bitcast.9, bf16[4,64,1536]{2,1,0:T(8,128)(2,1)} %bitcast.10, bf16[4,64,1536]{2,1,0:T(8,128)(2,1)} %bitcast.11, bf16[4,2,64,1536]{3,2,1,0:T(8,128)(2,1)} %bitcast.8), custom_call_target="tpu_custom_call" | custom-call | flops 4630511616 | bytes 6291456 | tf_op jit(solution)/shard_map/span_attention/pallas_call | solution.py:394
  69.1 0.9 %copy.9 = bf16[1,4,8,8,1536]{4,3,2,1,0:T(8,128)(2,1)} copy(bf16[1,4,8,8,1536]{4,3,2,1,0:T(8,128)(2,1)S(1)} %bitcast.7) | data formatting | bytes 1572864

commit v3 on v2

--- a/solution.py
+++ b/solution.py
@@ -22,6 +22,8 @@
 CHUNKS = 3
 CW = HD // CHUNKS
 LEAD = 3
+EARLY = 8
+LAST_LEAD = 2
 LAG = 2
 MERGE_LAG = 2
 FIRST_OWN = 5
@@ -82,6 +84,12 @@
             land.at[h, 0], land.at[h, 1 + way], own_ss.at[way, h], own_rs.at[way, h], (x_next, x_prev)[way]
         )
 
+    def own_first(h, way):
+        return remote(
+            cache_hbm.at[:, :, :, lanes(h)], land.at[h, 1 + way], own_ss.at[way, h], own_rs.at[way, h],
+            (x_next, x_prev)[way],
+        )
+
     def forward(h, way):
         half = pl.ds(2 * way, 2)
         return remote(
@@ -136,6 +144,15 @@
     k_copy.start()
     v_copy.start()
     lax.fori_loop(LEAD, HEADS, start_local, 0)
+
+    neighbours = [jnp.where(has, 1, 0) for has in row_has + col_has]
+    pl.semaphore_wait(barrier, 3 + sum(neighbours))
+    for h in range(LEAD):
+        own_first(h, 0).start()
+        own_first(h, 1).start()
+    for h in range(LEAD):
+        q_copy(h).wait()
+        q_send(h).start()
 
     place = lax.broadcasted_iota(jnp.int32, (16, QN), 0)
     source = place >> 2
@@ -150,16 +167,9 @@
             count = count + jnp.where(target == listed, 1, 0)
         ref[...] = jnp.where(count == 0, NONE, jnp.where(count == 1, 0.0, TWICE)).astype(jnp.float32)
 
-    neighbours = [jnp.where(has, 1, 0) for has in row_has + col_has]
-    pl.semaphore_wait(barrier, 3 + sum(neighbours))
+    bias_send.start()
     for h in range(LEAD):
         cache_copy(h).wait()
-        own_send(h, 0).start()
-        own_send(h, 1).start()
-        q_copy(h).wait()
-        q_send(h).start()
-        if h == 0:
-            bias_send.start()
     k_copy.wait()
     v_copy.wait()
     for c in range(CHUNKS):
@@ -318,11 +328,16 @@
                 own_send(h, way).wait_recv()
                 forward(h, way).start()
 
+        def send_step(i, carry):
+            cache_copy(i).wait()
+            own_send(i, 0).start()
+            own_send(i, 1).start()
+            return carry
+
+        lax.fori_loop(sent(h), sent(h + 1), send_step, 0)
+
         @pl.when(h + LEAD < HEADS)
         def _():
-            cache_copy(h + LEAD).wait()
-            own_send(h + LEAD, 0).start()
-            own_send(h + LEAD, 1).start()
             q_copy(h + LEAD).wait()
             q_send(h + LEAD).start()
 
@@ -363,12 +378,16 @@
         lax.fori_loop(own_done(h), own_done(h + 1), own_step, 0)
         return carry
 
+    def sent(step):
+        return jnp.minimum(jnp.minimum(step + LEAD, jnp.maximum(EARLY, step + LAST_LEAD)), HEADS)
+
     def own_done(step):
-        return jnp.clip(2 * (step - FIRST_OWN), 0, jnp.maximum(step - LAG, 0))
+        caught_up = jnp.clip(2 * (step - FIRST_OWN), 0, jnp.maximum(step - LAG - 1, 0))
+        return jnp.where(step >= steps, HEADS, caught_up)
 
     steps = HEADS + LAG
     lax.fori_loop(0, steps, ring_step, 0)
-    for h in range(min(2 * (steps - MERGE_LAG - FIRST_OWN), HEADS - MERGE_LAG), HEADS):
+    for h in range(HEADS - MERGE_LAG - 1, HEADS - 1):
         merge(h)
 
     def finish(h, carry):
@@ -385,6 +404,7 @@
         for way in range(2):
             pl.when(row_to[way])(row_send(c, way).wait_send)
             pl.when(col_to[way])(col_send(c, way).wait_send)
+    merge(HEADS - 1)
 
 
 def per_device(queries, keys, values, cache, ctx_owner, ctx_slot, span_count):

time: 70 us -> 69.7 us (level)
  no operation moved by 1% of the time
where the time goes in v3:
time: 69.7 us; the launch traced here: 69.6 us
  Pallas kernels  68 us (98%)
  local copies, waits for them, and re-layouts  0.88 us (1%)
    pallas_call x1, Pallas kernels, per_device(): pl.pallas_call(kernel, out_shape=pltpu.VMEM((QN, HD), bf16), in_specs=[sm...  68 us

profile of v3, /device:TPU:96, one launch (start us, length us, event | category | flops | bytes accessed | tf_op | source)
XLA Modules:
  0.0 69.6 jit_solution(16562496824848903681)
XLA Ops:
  0.7 68.0 %span_attention.1 = bf16[256,1536]{1,0:T(8,128)(2,1)S(1)} custom-call(s32[8]{0:T(128)} %bitcast.12, s32[8]{0:T(128)} %bitcast.13, s32[1]{0:T(128)S(6)} %copy.10.span_ref, bf16[256,1536]{1,0:T(8,128)(2,1)} %bitcast.9, bf16[4,64,1536]{2,1,0:T(8,128)(2,1)} %bitcast.10, bf16[4,64,1536]{2,1,0:T(8,128)(2,1)} %bitcast.11, bf16[4,2,64,1536]{3,2,1,0:T(8,128)(2,1)} %bitcast.8), custom_call_target="tpu_custom_call" | custom-call | flops 4630511616 | bytes 6291456 | tf_op jit(solution)/shard_map/span_attention/pallas_call | solution.py:414
  68.7 0.9 %copy.9 = bf16[1,4,8,8,1536]{4,3,2,1,0:T(8,128)(2,1)} copy(bf16[1,4,8,8,1536]{4,3,2,1,0:T(8,128)(2,1)S(1)} %bitcast.7) | data formatting | bytes 1572864

commit v4 on v3

--- a/solution.py
+++ b/solution.py
@@ -26,7 +26,7 @@
 LAST_LEAD = 2
 LAG = 2
 MERGE_LAG = 2
-FIRST_OWN = 5
+FIRST_OWN = 6
 NONE = -1e30
 FLOOR = -(2.0**96)
 RATE = math.log2(math.e) / math.sqrt(HEAD)

time: 69.7 us -> 69.7 us (level)
  no operation moved by 1% of the time
where the time goes in v4:
time: 69.7 us; the launch traced here: 69.6 us
  Pallas kernels  68 us (98%)
  local copies, waits for them, and re-layouts  0.88 us (1%)
    pallas_call x1, Pallas kernels, per_device(): pl.pallas_call(kernel, out_shape=pltpu.VMEM((QN, HD), bf16), in_specs=[sm...  68 us

profile of v4, /device:TPU:96, one launch (start us, length us, event | category | flops | bytes accessed | tf_op | source)
XLA Modules:
  0.0 69.6 jit_solution(17746838900157736867)
XLA Ops:
  0.7 68.0 %span_attention.1 = bf16[256,1536]{1,0:T(8,128)(2,1)S(1)} custom-call(s32[8]{0:T(128)} %bitcast.12, s32[8]{0:T(128)} %bitcast.13, s32[1]{0:T(128)S(6)} %copy.10.span_ref, bf16[256,1536]{1,0:T(8,128)(2,1)} %bitcast.9, bf16[4,64,1536]{2,1,0:T(8,128)(2,1)} %bitcast.10, bf16[4,64,1536]{2,1,0:T(8,128)(2,1)} %bitcast.11, bf16[4,2,64,1536]{3,2,1,0:T(8,128)(2,1)} %bitcast.8), custom_call_target="tpu_custom_call" | custom-call | flops 4630511616 | bytes 6291456 | tf_op jit(solution)/shard_map/span_attention/pallas_call | solution.py:414
  68.7 0.9 %copy.9 = bf16[1,4,8,8,1536]{4,3,2,1,0:T(8,128)(2,1)} copy(bf16[1,4,8,8,1536]{4,3,2,1,0:T(8,128)(2,1)S(1)} %bitcast.7) | data formatting | bytes 1572864
